TPU v7x, 32 devices: a whole 2x2x4 slice. The times are simulated.
32 devices in a mesh: hours: 8 (over y, x, core), blocks: 4 (over z).
Axes of the slice: x: 2, y: 2, z: 4, core: 2. Of those that a mesh axis runs over, the one named last changes fastest.
Arguments:
- spectra: float32 [8, 64, 3, 2, 2048], P('hours', 'blocks'), may hold values from -6 to 6
- validity: int32 [8, 64], P('hours', 'blocks'), may hold values from 0 to 1, as said below
Outputs:
- near_stack: float32 [4, 2, 2304, 256], P('blocks', None, 'hours')
- far_stack: float32 [4, 1152, 256], P('blocks', 'hours')
Inputs may be any that keep to these rules, and one draw needn't show every extreme that they name: `validity`: 0 or 1; some stations are invalid in every hour.
All inputs are finite; a program needn't handle non-finite values.
Results may differ from a plain program's by a relative error of at most 0.0058.
Values may be sent and summed in bfloat16 or wider, within the bound.
A program may use at most 64 MiB of HBM per device.

v0:
```python
import math

import jax
import jax.numpy as jnp
from jax import lax
from jax.sharding import PartitionSpec as P

BAND = 128
LAGS = 256


EPSILON = 1e-06


def passed_along(block, axis, distance):
    devices = range(lax.axis_size(axis))
    route = [((i - distance) % len(devices), i) for i in devices]
    return lax.ppermute(block, axis, route)


def whiten(spectra, validity, band_width):
    hour_count, station_count, comp_count, part_count, freq_count = spectra.shape
    grouped = spectra.reshape(
        hour_count, station_count, comp_count, part_count, freq_count // band_width, band_width
    )
    band_power = jnp.mean(grouped * grouped, axis=(3, 5), keepdims=True)
    valid_f = validity.astype(jnp.float32).reshape(hour_count, station_count, 1, 1, 1, 1)
    scaled = grouped * (valid_f / jnp.sqrt(band_power + EPSILON))
    return scaled.reshape(hour_count, station_count * comp_count, part_count, freq_count).astype(
        jnp.bfloat16
    )


def build_table(freq_count, lag_count):
    freq_index = jnp.arange(freq_count, dtype=jnp.int32)[:, None]
    lag_index = jnp.arange(lag_count, dtype=jnp.int32)[None, :] - lag_count // 2
    residue = freq_index * (lag_index + 2 * freq_count) % (2 * freq_count)
    angles = residue.astype(jnp.float32) * (math.pi / freq_count)
    amplitude = 8.0 / math.sqrt(freq_count)
    return jnp.concatenate([jnp.cos(angles) * amplitude, -jnp.sin(angles) * amplitude], 0).astype(
        jnp.bfloat16
    )


def cross_spectrum(row_block, col_block):
    row_real = row_block[..., :, None, 0, :].astype(jnp.float32)
    row_imag = row_block[..., :, None, 1, :].astype(jnp.float32)
    col_real = col_block[..., None, :, 0, :].astype(jnp.float32)
    col_imag = col_block[..., None, :, 1, :].astype(jnp.float32)
    real_part = row_real * col_real + row_imag * col_imag
    imag_part = row_imag * col_real - row_real * col_imag
    stacked_parts = jnp.stack([real_part, imag_part], -2)
    dims_shape = stacked_parts.shape
    return stacked_parts.reshape(
        dims_shape[:-4] + (dims_shape[-4] * dims_shape[-3], dims_shape[-2] * dims_shape[-1])
    ).astype(jnp.bfloat16)


def expand(counts, comp_count):
    return jnp.repeat(jnp.repeat(counts, comp_count, 0), comp_count, 1).reshape(-1)


def correlate(row_block, col_block, table):
    hour_count, row_count, part_count, freq_count = row_block.shape
    trace_count = col_block.shape[1]
    row_step = 4
    grouped = row_block.reshape(
        hour_count, row_count // row_step, row_step, part_count, freq_count
    ).transpose(1, 0, 2, 3, 4)

    def one_block(sub_rows):
        spectrum = cross_spectrum(sub_rows, col_block)
        return jnp.einsum("hpk,kl->pl", spectrum, table, preferred_element_type=jnp.float32)

    result = lax.map(one_block, grouped)
    return result.reshape(row_count * trace_count, table.shape[1])


def on_device(spectra, validity):
    hour_count, station_count, comp_count, part_count, freq_count = spectra.shape
    trace_count = station_count * comp_count
    half_width = trace_count // 2
    half_stations = station_count // 2
    white = whiten(spectra, validity, BAND)
    table = build_table(freq_count, LAGS)
    valid_wire = validity.astype(jnp.bfloat16)
    block_count = lax.axis_size("blocks")
    near_rounds = block_count // 2
    my_block = lax.axis_index("blocks")
    is_lower = my_block < near_rounds
    panels = [(white, valid_wire)]
    for round_index in range(1, near_rounds + 1):
        panels.append(passed_along((white, valid_wire), "blocks", round_index))
    near_terms = jnp.stack(
        [correlate(white, panels[round_index][0], table) for round_index in range(near_rounds)], 0
    )
    far_white, far_valid = panels[near_rounds]
    far_rows = jnp.where(is_lower, white[:, :half_width], far_white[:, half_width:])
    far_cols = jnp.where(is_lower, far_white, white)
    far_terms = correlate(far_rows, far_cols, table)
    hour_devices = lax.axis_size("hours")
    share_near = trace_count * trace_count // hour_devices
    share_far = half_width * trace_count // hour_devices
    my_slot = lax.axis_index("hours")
    hour_masks = lax.all_gather(validity, "hours", axis=0, tiled=True)
    all_masks = lax.all_gather(hour_masks, "blocks", axis=1, tiled=True).astype(jnp.float32)
    pair_counts = jnp.dot(
        all_masks.T, all_masks, precision=lax.Precision.HIGHEST, preferred_element_type=jnp.float32
    )
    near_sum, far_sum = (
        lax.psum_scatter(near_terms, "hours", scatter_dimension=1, tiled=True),
        lax.psum_scatter(far_terms, "hours", scatter_dimension=0, tiled=True),
    )

    def block_count_of(row_start, row_count, col_start):
        sub_block = lax.dynamic_slice(
            pair_counts, (row_start, col_start), (row_count, station_count)
        )
        return expand(sub_block, comp_count)

    near_full = jnp.stack(
        [
            block_count_of(
                my_block * station_count,
                station_count,
                (my_block - round_index) % block_count * station_count,
            )
            for round_index in range(near_rounds)
        ],
        0,
    )
    far_partner = (my_block + near_rounds) % block_count
    far_full = block_count_of(
        jnp.where(is_lower, my_block * station_count, far_partner * station_count + half_stations),
        half_stations,
        jnp.where(is_lower, far_partner, my_block) * station_count,
    )
    near_count = lax.dynamic_slice_in_dim(near_full, my_slot * share_near, share_near, 1)
    far_count = lax.dynamic_slice_in_dim(far_full, my_slot * share_far, share_far, 0)
    near_stack = near_sum / jnp.maximum(near_count, 1.0)[..., None]
    far_stack = far_sum / jnp.maximum(far_count, 1.0)[..., None]
    return (near_stack[None], far_stack[None])


def solution(mesh):
    in_specs = (P("hours", "blocks", None, None, None), P("hours", "blocks"))
    out_specs = (P("blocks", None, "hours", None), P("blocks", "hours", None))
    return jax.shard_map(
        on_device, mesh=mesh, in_specs=in_specs, out_specs=out_specs, check_vma=False
    )
```

profile of v0, /device:TPU:0, one launch (start us, length us, event | category | flops | bytes accessed | tf_op | source)
XLA Modules:
  0.0 428.7 jit_solution(7965493983117222628)
XLA Ops:
  12.4 4.0 collective-permute-start.1
  18.2 8.7 %multiply_convert_fusion.1 = (bf16[2048,256]{1,0:T(8,128)(2,1)S(1)}, bf16[2048,256]{1,0:T(8,128)(2,1)S(1)}) fusion(s32[256]{0:T(256)S(1)} %iota_add_fusion), kind=kLoop, calls=%fused_computation.51 | loop fusion | flops 9961472 | bytes 2098176 | tf_op jit(solution)/shard_map/convert.18
  29.8 141.1 %while.30 = (s32[]{:T(128)}, f32[12,192,256]{2,1,0:T(8,128)S(1)}, bf16[12,1,4,2,2048]{4,3,2,1,0:T(2,128)(2,1)}, bf16[1,48,2,2048]{3,2,1,0:T(2,128)(2,1)}, bf16[4096,256]{1,0:T(8,128)(2,1)}, /*index=5*/s32[]{:T(128)}) while((s32[]{:T(128)}, f32[12,192,256]{2,1,0:T(8,128)S(1)}, bf16[12,1,4,2,2048]{4,3,2,1,0:T(2,128)(2,1)}, ...), condition=%wide.region_3.4_spmd, body=%wide.region_2.3_spmd.sunk | while | flops 409157632 | bytes 24019056 | solution.py:75
  32.7 3.3 add_convert_fusion.6
  36.0 3.3 pad_maximum_fusion.8
  44.5 3.3 add_convert_fusion.6
  47.8 3.3 pad_maximum_fusion.8
  56.2 3.3 add_convert_fusion.6
  59.5 3.3 pad_maximum_fusion.8
  68.0 3.3 add_convert_fusion.6
  71.3 3.3 pad_maximum_fusion.8
  79.8 3.3 add_convert_fusion.6
  83.1 3.3 pad_maximum_fusion.8
  91.5 3.3 add_convert_fusion.6
  94.8 3.3 pad_maximum_fusion.8
  103.3 3.3 add_convert_fusion.6
  106.6 3.3 pad_maximum_fusion.8
  115.0 3.3 add_convert_fusion.6
  118.4 3.3 pad_maximum_fusion.8
  126.8 3.3 add_convert_fusion.6
  130.1 3.3 pad_maximum_fusion.8
  138.6 3.3 add_convert_fusion.6
  141.9 3.3 pad_maximum_fusion.8
  150.3 3.3 add_convert_fusion.6
  153.6 3.3 pad_maximum_fusion.8
  162.1 3.3 add_convert_fusion.6
  165.4 3.3 pad_maximum_fusion.8
  175.4 58.6 %while.32 = (s32[]{:T(128)}, f32[6,192,256]{2,1,0:T(8,128)S(1)}, bf16[6,1,4,2,2048]{4,3,2,1,0:T(2,128)(2,1)S(1)}, bf16[1,48,2,2048]{3,2,1,0:T(2,128)(2,1)S(1)}, bf16[4096,256]{1,0:T(8,128)(2,1)}, /*index=5*/s32[]{:T(128)}) while((s32[]{:T(128)}, f32[6,192,256]{2,1,0:T(8,128)S(1)}, bf16[6,1,4,2,2048]{4,3,2,1,0:T(2,128)(2,1)S(1)}, ...), condition=%wide.region_8.9_spmd, body=%wide.region_7.8_spmd.sunk | while | flops 409157632 | bytes 24019056 | solution.py:75
  176.3 3.3 add_convert_fusion.8
  179.6 3.3 pad_maximum_fusion.10
  186.1 3.3 add_convert_fusion.8
  189.4 3.3 pad_maximum_fusion.10
  195.8 3.3 add_convert_fusion.8
  199.2 3.3 pad_maximum_fusion.10
  205.6 3.3 add_convert_fusion.8
  208.9 3.3 pad_maximum_fusion.10
  215.4 3.3 add_convert_fusion.8
  218.7 3.3 pad_maximum_fusion.10
  225.1 3.3 add_convert_fusion.8
  228.4 3.3 pad_maximum_fusion.10
  235.6 126.5 %while.31 = (s32[]{:T(128)}, f32[12,192,256]{2,1,0:T(8,128)S(1)}, bf16[12,1,4,2,2048]{4,3,2,1,0:T(2,128)(2,1)}, bf16[1,48,2,2048]{3,2,1,0:T(2,128)(2,1)S(1)}, bf16[4096,256]{1,0:T(8,128)(2,1)}, /*index=5*/s32[]{:T(128)}) while((s32[]{:T(128)}, f32[12,192,256]{2,1,0:T(8,128)S(1)}, bf16[12,1,4,2,2048]{4,3,2,1,0:T(2,128)(2,1)}, ...), condition=%wide.region_5.6_spmd, body=%wide.region_4.5_spmd.sunk | while | flops 409157632 | bytes 24019056 | solution.py:75
  237.2 3.3 add_convert_fusion.7
  240.6 3.3 pad_maximum_fusion.9
  251.1 3.3 pad_maximum_fusion.9
  261.8 3.3 pad_maximum_fusion.9
  269.0 3.3 add_convert_fusion.7
  272.4 3.3 pad_maximum_fusion.9
  279.6 3.3 add_convert_fusion.7
  282.9 3.3 pad_maximum_fusion.9
  293.4 3.3 pad_maximum_fusion.9
  300.6 3.3 add_convert_fusion.7
  303.9 3.3 pad_maximum_fusion.9
  311.1 3.3 add_convert_fusion.7
  314.4 3.3 pad_maximum_fusion.9
  324.9 3.3 pad_maximum_fusion.9
  335.5 3.3 pad_maximum_fusion.9
  342.7 3.3 add_convert_fusion.7
  346.0 3.3 pad_maximum_fusion.9
  353.2 3.3 add_convert_fusion.7
  356.5 3.3 pad_maximum_fusion.9
  362.0 4.1 pad_maximum_fusion.3
  366.8 8.7 %all-gather = s32[8,1,16]{2,1,0:T(1,128)S(1)} all-gather(s32[1,1,16]{2,1,0:T(1,128)S(1)} %bitcast.151), channel_id=1, replica_groups=mesh['hours'=8,'blocks'=4] {'hours'}, dimensions={0}, use_global_device_ids=true | all-gather | bytes 576 | tf_op jit(solution)/shard_map/all_gather | solution.py:105
  375.5 13.1 %all-gather.1 = s32[4,16,8]{1,2,0:T(8,128)S(1)} all-gather(s32[1,16,8]{1,2,0:T(8,128)S(1)} %bitcast.150), channel_id=1, replica_groups=mesh['hours'=8,'blocks'=4] {'blocks'}, dimensions={0}, use_global_device_ids=true | all-gather | bytes 2560 | tf_op jit(solution)/shard_map/all_gather | solution.py:106
  392.3 27.5 %reduce-scatter.3.cloned.1.call-done = f32[2,288,256]{2,1,0:T(8,128)} async-done(((f32[2,2304,256]{2,1,0:T(8,128)}), f32[2,288,256]{2,1,0:T(8,128)}) %reduce-scatter.3.cloned.1.call-update) | async-done | bytes 589840 | tf_op jit(solution)/shard_map/reduce_scatter | solution.py:111
  (335 shorter events, 163.4 us)
Async XLA Ops:
  7.2 383.4 %reduce-scatter.5.cloned.1.call-start = ((), (), s32[]{:S(2)}) async-start(), calls=%async_computation.3 | async-start | bytes 1327104 | tf_op jit(solution)/shard_map/reduce_scatter | solution.py:112
  10.2 1.1 copy-start
  11.0 1.4 copy-start.2
  12.4 159.9 %collective-permute-start.1 = (bf16[1,48,2,2048]{3,2,1,0:T(2,128)(2,1)}, bf16[1,48,2,2048]{3,2,1,0:T(2,128)(2,1)}, u32[]{:S(2)}, u32[]{:S(2)}) collective-permute-start(bf16[1,48,2,2048]{3,2,1,0:T(2,128)(2,1)} %multiply_convert_fusion.2), channel_id=1, source_target_pairs={{2,0},{3,1},{0,2},{1,3},{6,4},{7,5},{4,6},{5,7},{10,8},{11,9},{8,1... | collective-permute-start | bytes 1179656 | tf_op jit(solution)/shard_map/ppermute | solution.py:18
  16.5 218.9 %collective-permute-start = (bf16[1,48,2,2048]{3,2,1,0:T(2,128)(2,1)}, bf16[1,48,2,2048]{3,2,1,0:T(2,128)(2,1)S(1)}, u32[]{:S(2)}, u32[]{:S(2)}) collective-permute-start(bf16[1,48,2,2048]{3,2,1,0:T(2,128)(2,1)} %multiply_convert_fusion.2), channel_id=1, source_target_pairs={{3,0},{0,1},{1,2},{2,3},{7,4},{4,5},{5,6},{6,7},{11,8},{8,9},{9,10... | collective-permute-start | bytes 1179656 | tf_op jit(solution)/shard_map/ppermute | solution.py:18
  39.4 1.6 copy-start.3
  51.1 1.6 copy-start.3
  62.9 1.6 copy-start.3
  74.6 1.6 copy-start.3
  86.4 1.6 copy-start.3
  98.2 1.6 copy-start.3
  109.9 1.6 copy-start.3
  121.7 1.6 copy-start.3
  133.5 1.6 copy-start.3
  145.2 1.6 copy-start.3
  157.0 1.6 copy-start.3
  168.7 1.6 copy-start.3
  170.9 1.4 copy-start.1
  172.4 3.0 copy-start.6
  183.0 1.6 copy-start.4
  192.7 1.6 copy-start.4
  202.5 1.6 copy-start.4
  212.2 1.6 copy-start.4
  222.0 1.6 copy-start.4
  231.8 1.6 copy-start.4
  234.0 1.1 copy-start.7
  235.1 184.7 %reduce-scatter.3.cloned.1.call-start = ((), (), s32[]{:S(2)}) async-start(), calls=%async_computation.2 | async-start | bytes 5308416 | tf_op jit(solution)/shard_map/reduce_scatter | solution.py:111
  243.9 1.6 copy-start.5
  254.5 1.8 copy-start.5
  265.2 1.6 copy-start.5
  275.7 1.6 copy-start.5
  286.2 1.6 copy-start.5
  296.7 1.6 copy-start.5
  307.2 1.6 copy-start.5
  317.8 1.6 copy-start.5
  328.3 1.6 copy-start.5
  338.8 1.6 copy-start.5
  349.3 1.6 copy-start.5
  359.8 1.6 copy-start.5
  366.1 0.7 copy-start.8
Sparse Core Ops, SparseCore 0:
  235.2 36.5 reduce-scatter.4
  366.3 53.4 reduce-scatter.2
where the time goes:
time: 432 us; the launch traced here: 429 us
  other arithmetic  258 us (60%)
  local copies, waits for them, and re-layouts  80.9 us (19%)
  waiting for transfers between devices  27.6 us (6%)
  blocking collectives  21.8 us (5%)
  matrix products  17.5 us (4%)
  between operations  14.3 us (3%)
  starting transfers between devices  5.91 us (1%)
    another operation x31, other arithmetic  108 us
    another operation x30, other arithmetic, cross_spectrum(): stacked_parts = jnp.stack([real_part, imag_part], -2)  99.6 us
    while x150, local copies, waits for them, and re-layouts  55.9 us
    convert_element_type x30, other arithmetic, cross_spectrum(): col_real = col_block[..., None, :, 0, :].astype(jnp.float32)  31.3 us
    reduce_scatter x1, waiting for transfers between devices, on_device(): lax.psum_scatter(near_terms, 'hours', scatter_dimension=1, tiled=True)  27.5 us
    squeeze x30, local copies, waits for them, and re-layouts, correlate(): result = lax.map(one_block, grouped)  19.1 us
    dot_general x30, matrix products, one_block(): jnp.einsum('hpk,kl->pl', spectrum, table, preferred_element_type=jnp.floa...  17.3 us
    all_gather x1, blocking collectives, on_device(): lax.all_gather(hour_masks, 'blocks', axis=1, tiled=True).astype(jnp.float32)  13.1 us
  transfers between devices with their start and end apart: 4, of which 1 were waited for; matrix products, arithmetic and copies ran while one was open for 74% of the time, Pallas kernels for 0%

commit v1 on v0

v1 whole, which is shorter than its diff:
```python
import functools
import math

import jax
import jax.numpy as jnp
import ml_dtypes
import numpy as np
from jax import lax
from jax.experimental import pallas as pl
from jax.experimental.pallas import tpu as pltpu
from jax.sharding import PartitionSpec as P

BAND = 128
LAGS = 256
EPSILON = 1e-06
CHUNK = 256


def passed_along(block, axis, distance):
    devices = range(lax.axis_size(axis))
    route = [((i - distance) % len(devices), i) for i in devices]
    return lax.ppermute(block, axis, route)


def chunked_table(freq_count, lag_count):
    freq = np.arange(freq_count, dtype=np.int64)[:, None]
    lag = np.arange(lag_count, dtype=np.int64)[None, :] - lag_count // 2
    angles = ((freq * lag) % (2 * freq_count)).astype(np.float64) * (math.pi / freq_count)
    amplitude = 8.0 / math.sqrt(freq_count)
    parts = np.stack([np.cos(angles) * amplitude, -np.sin(angles) * amplitude], 0)
    parts = parts.reshape(2, freq_count // CHUNK, CHUNK, lag_count).transpose(1, 0, 2, 3)
    return parts.reshape(2 * freq_count, lag_count).astype(np.float32).astype(ml_dtypes.bfloat16)


def whiten_into(spectra_ref, valid_ref, store):
    freq_count = spectra_ref.shape[2]
    valid = valid_ref[...]
    for band in range(freq_count // BAND):
        lanes = slice(band * BAND, (band + 1) * BAND)
        real = spectra_ref[:, 0, lanes]
        imag = spectra_ref[:, 1, lanes]
        total = jnp.sum(real * real + imag * imag, axis=1, keepdims=True)
        scale = valid / jnp.sqrt(total * (1.0 / (2 * BAND)) + EPSILON)
        store(0, lanes, (real * scale).astype(jnp.bfloat16))
        store(1, lanes, (imag * scale).astype(jnp.bfloat16))


def whiten_kernel(spectra_ref, valid_ref, white_ref):
    def store(part, lanes, value):
        white_ref[part, :, lanes] = value

    whiten_into(spectra_ref, valid_ref, store)


def cross_chunk(rows_ref, row_start, row_count, cols_ref, panel, chunk, out_ref):
    col_count = cols_ref.shape[2]
    lanes = pl.ds(chunk * CHUNK, CHUNK)
    cols = [
        (
            cols_ref[panel, 0, q : q + 16, lanes],
            cols_ref[panel, 1, q : q + 16, lanes],
        )
        for q in range(0, col_count, 16)
    ]
    for a in range(row_count):
        row_real = jnp.broadcast_to(rows_ref[0, pl.ds(row_start + a, 1), lanes], (16, CHUNK))
        row_imag = jnp.broadcast_to(rows_ref[1, pl.ds(row_start + a, 1), lanes], (16, CHUNK))
        row_real = row_real.astype(jnp.bfloat16)
        row_imag = row_imag.astype(jnp.bfloat16)
        for q, (col_real, col_imag) in enumerate(cols):
            at = slice(a * col_count + q * 16, a * col_count + q * 16 + 16)
            out_ref[at, :CHUNK] = row_real * col_real + row_imag * col_imag
            out_ref[at, CHUNK:] = row_imag * col_real - row_real * col_imag


def correlate_unit(rows_ref, row_start, row_count, cols_ref, panel, table_ref, acc_ref, tiles):
    chunk_count = rows_ref.shape[2] // CHUNK
    cross = functools.partial(cross_chunk, rows_ref, row_start, row_count, cols_ref, panel)
    cross(0, tiles[0])
    for chunk in range(chunk_count):
        if chunk + 1 < chunk_count:
            cross(chunk + 1, tiles[(chunk + 1) % 2])
        term = jnp.dot(
            tiles[chunk % 2][...],
            table_ref[chunk * 2 * CHUNK : (chunk + 1) * 2 * CHUNK, :],
            preferred_element_type=jnp.float32,
        )
        if chunk == 0:
            acc_ref[...] = term
        else:
            acc_ref[...] += term


def correlate_kernel(block_count, white_ref, table_ref, out_ref, rows, tile0, tile1):
    trace_count = white_ref.shape[2]
    half = trace_count // 2
    is_lower = lax.axis_index("blocks") < block_count // 2
    rows[:, :trace_count, :] = white_ref[0].astype(jnp.float32)
    far_own = white_ref[0, :, :, :].astype(jnp.float32)[:, :half]
    far_other = white_ref[2, :, :, :].astype(jnp.float32)[:, half:]
    rows[:, trace_count:, :] = jnp.where(is_lower, far_own, far_other)

    def one_unit(unit, carry):
        near = unit < 4
        row_start = jnp.where(near, lax.rem(unit, 2) * half, trace_count)
        panel = jnp.where(near, unit // 2, jnp.where(is_lower, 2, 0))
        correlate_unit(
            rows, row_start, half, white_ref, panel, table_ref, out_ref.at[unit], (tile0, tile1)
        )
        return carry

    lax.fori_loop(0, 5, one_unit, 0)


def expand(counts, comp_count):
    return jnp.repeat(jnp.repeat(counts, comp_count, 0), comp_count, 1).reshape(-1)


def on_device(table, spectra, validity):
    hour_count, station_count, comp_count, part_count, freq_count = spectra.shape
    trace_count = station_count * comp_count
    half_width = trace_count // 2
    half_stations = station_count // 2
    block_count = lax.axis_size("blocks")
    near_rounds = block_count // 2
    my_block = lax.axis_index("blocks")
    is_lower = my_block < near_rounds
    valid_f = jnp.repeat(validity.reshape(-1).astype(jnp.float32), comp_count)[:, None]
    white = pl.pallas_call(
        whiten_kernel,
        out_shape=jax.ShapeDtypeStruct((part_count, trace_count, freq_count), jnp.bfloat16),
        in_specs=[pl.BlockSpec(memory_space=pltpu.VMEM)] * 2,
        out_specs=pl.BlockSpec(memory_space=pltpu.VMEM),
    )(spectra.reshape(trace_count, part_count, freq_count), valid_f)
    panels = [white] + [passed_along(white, "blocks", r) for r in range(1, near_rounds + 1)]
    pair_rows = half_width * trace_count
    sums = pl.pallas_call(
        functools.partial(correlate_kernel, block_count),
        out_shape=jax.ShapeDtypeStruct((5, pair_rows, LAGS), jnp.float32),
        in_specs=[pl.BlockSpec(memory_space=pltpu.VMEM)] * 2,
        out_specs=pl.BlockSpec(memory_space=pltpu.VMEM),
        scratch_shapes=[
            pltpu.VMEM((part_count, trace_count + half_width, freq_count), jnp.float32),
            pltpu.VMEM((pair_rows, 2 * CHUNK), jnp.bfloat16),
            pltpu.VMEM((pair_rows, 2 * CHUNK), jnp.bfloat16),
        ],
        compiler_params=pltpu.CompilerParams(vmem_limit_bytes=56 * 1024 * 1024),
    )(jnp.stack(panels, 0), table)
    near_terms = sums[:4].reshape(near_rounds, 2 * pair_rows, LAGS)
    far_terms = sums[4]
    hour_devices = lax.axis_size("hours")
    share_near = trace_count * trace_count // hour_devices
    share_far = half_width * trace_count // hour_devices
    my_slot = lax.axis_index("hours")
    hour_masks = lax.all_gather(validity, "hours", axis=0, tiled=True)
    all_masks = lax.all_gather(hour_masks, "blocks", axis=1, tiled=True).astype(jnp.float32)
    pair_counts = jnp.dot(
        all_masks.T, all_masks, precision=lax.Precision.HIGHEST, preferred_element_type=jnp.float32
    )
    near_sum, far_sum = (
        lax.psum_scatter(near_terms, "hours", scatter_dimension=1, tiled=True),
        lax.psum_scatter(far_terms, "hours", scatter_dimension=0, tiled=True),
    )

    def block_count_of(row_start, row_count, col_start):
        sub_block = lax.dynamic_slice(
            pair_counts, (row_start, col_start), (row_count, station_count)
        )
        return expand(sub_block, comp_count)

    near_full = jnp.stack(
        [
            block_count_of(
                my_block * station_count,
                station_count,
                (my_block - round_index) % block_count * station_count,
            )
            for round_index in range(near_rounds)
        ],
        0,
    )
    far_partner = (my_block + near_rounds) % block_count
    far_full = block_count_of(
        jnp.where(is_lower, my_block * station_count, far_partner * station_count + half_stations),
        half_stations,
        jnp.where(is_lower, far_partner, my_block) * station_count,
    )
    near_count = lax.dynamic_slice_in_dim(near_full, my_slot * share_near, share_near, 1)
    far_count = lax.dynamic_slice_in_dim(far_full, my_slot * share_far, share_far, 0)
    near_stack = near_sum / jnp.maximum(near_count, 1.0)[..., None]
    far_stack = far_sum / jnp.maximum(far_count, 1.0)[..., None]
    return (near_stack[None], far_stack[None])


def solution(mesh):
    in_specs = (P("hours", "blocks", None, None, None), P("hours", "blocks"))
    out_specs = (P("blocks", None, "hours", None), P("blocks", "hours", None))

    def run(spectra, validity):
        table = chunked_table(spectra.shape[-1], LAGS)
        return jax.shard_map(
            lambda *args: on_device(jnp.asarray(table), *args),
            mesh=mesh, in_specs=in_specs, out_specs=out_specs, check_vma=False,
        )(spectra, validity)

    return run
```

time: 432 us -> 169 us (0.39)
  other arithmetic: 258 us -> 6.66 us
  local copies, waits for them, and re-layouts: 80.9 us -> 10.1 us
  waiting for transfers between devices: 27.6 us -> 88.3 us
  Pallas kernels: 0 us -> 21 us
  matrix products: 17.5 us -> 0.24 us
    another operation x62 -> x1, other arithmetic: 212 us -> 2.14 us  [on_device(): jnp.stack(panels, 0)]
    while x150 -> x0, local copies, waits for them, and re-layouts: 55.9 us -> none
    convert_element_type x32 -> x1, other arithmetic: 33.6 us -> 0.66 us  [on_device(): validity.reshape(-1).astype(jnp.float32)]
    reduce_scatter x1, waiting for transfers between devices: 27.5 us -> 56.1 us  [on_device(): lax.psum_scatter(near_terms, 'hours', scatter_dimension=1, tiled=True)]
    ppermute x2, waiting for transfers between devices: 0.01 us -> 24.6 us  [passed_along(): return lax.ppermute(block, axis, route)]
    pallas_call x0 -> x2, Pallas kernels: none -> 21 us  [the longest x1 17.6 us: on_device(): pl.pallas_call(functools.partial(correlate_kernel, block_count), out_shap...]
    dot_general x30 -> x0, matrix products: 17.3 us -> none  [one_block(): jnp.einsum('hpk,kl->pl', spectrum, table, preferred_element_type=jnp.floa...]
    squeeze x30 -> x1, local copies, waits for them, and re-layouts: 19.1 us -> 2.38 us  [on_device(): far_terms = sums[4]]
  transfers between devices with their start and end apart: 4 -> 4, of which waited for: 1 -> 3; matrix products, arithmetic and copies ran while one was open for 74% -> 5% of each run, Pallas kernels for 0% -> 0%
where the time goes in v1:
time: 169 us; the launch traced here: 168 us
  waiting for transfers between devices  88.3 us (52%)
  blocking collectives  22.1 us (13%)
  Pallas kernels  21 us (12%)
  between operations  14.2 us (8%)
  local copies, waits for them, and re-layouts  10.1 us (6%)
  other arithmetic  6.66 us (4%)
  starting transfers between devices  5.69 us (3%)
    reduce_scatter x1, waiting for transfers between devices, on_device(): lax.psum_scatter(near_terms, 'hours', scatter_dimension=1, tiled=True)  56.1 us
    ppermute x2, waiting for transfers between devices, passed_along(): return lax.ppermute(block, axis, route)  24.6 us
    pallas_call x1, Pallas kernels, on_device(): pl.pallas_call(functools.partial(correlate_kernel, block_count), out_shap...  17.6 us
    all_gather x1, blocking collectives, on_device(): lax.all_gather(hour_masks, 'blocks', axis=1, tiled=True).astype(jnp.float32)  13.4 us
    all_gather x1, blocking collectives, on_device(): hour_masks = lax.all_gather(validity, 'hours', axis=0, tiled=True)  8.79 us
    reduce_scatter x1, waiting for transfers between devices, on_device(): lax.psum_scatter(far_terms, 'hours', scatter_dimension=0, tiled=True)  7.56 us
    ppermute x2, starting transfers between devices, passed_along(): return lax.ppermute(block, axis, route)  5.61 us
    slice x1, local copies, waits for them, and re-layouts, on_device(): near_terms = sums[:4].reshape(near_rounds, 2 * pair_rows, LAGS)  4.82 us
  transfers between devices with their start and end apart: 4, of which 3 were waited for; matrix products, arithmetic and copies ran while one was open for 5% of the time, Pallas kernels for 0%

profile of v1, /device:TPU:0, one launch (start us, length us, event | category | flops | bytes accessed | tf_op | source)
XLA Modules:
  0.0 168.2 jit_solution(3525140256668410909)
XLA Ops:
  7.2 0.0 reduce-scatter.5.cloned.1.call-start
  7.2 0.7 convert_bitcast_fusion
  7.9 0.1 broadcast_in_dim.29
  7.9 0.7 broadcast_in_dim_reshape.4.valid_ref
  8.6 3.3 %shard_map.50 = bf16[2,48,2048]{2,1,0:T(8,128)(2,1)} custom-call(f32[48,2,2048]{2,1,0:T(2,128)} %bitcast.25, f32[48,1]{1,0:T(8,128)} %broadcast_in_dim_reshape.4.valid_ref), custom_call_target="tpu_custom_call" | custom-call | tf_op jit(solution)/shard_map/pallas_call | solution.py:129
  12.0 4.0 %collective-permute-start.1 = (bf16[2,48,2048]{2,1,0:T(8,128)(2,1)}, bf16[2,48,2048]{2,1,0:T(8,128)(2,1)S(1)}, u32[]{:S(2)}, u32[]{:S(2)}) collective-permute-start(bf16[2,48,2048]{2,1,0:T(8,128)(2,1)} %shard_map.50), channel_id=1, source_target_pairs={{2,0},{3,1},{0,2},{1,3},{6,4},{7,5},{4,6},{5,7},{10,8},{11,9},{8,1... | collective-permute-start | bytes 1179656 | tf_op jit(solution)/shard_map/ppermute | solution.py:22
  16.0 1.6 collective-permute-start
  17.6 24.6 %collective-permute-done.1 = bf16[2,48,2048]{2,1,0:T(8,128)(2,1)S(1)} collective-permute-done((bf16[2,48,2048]{2,1,0:T(8,128)(2,1)}, bf16[2,48,2048]{2,1,0:T(8,128)(2,1)S(1)}, u32[]{:S(2)}, u32[]{:S(2)}) %collective-permute-start.1) | collective-permute-done | bytes 393248 | tf_op jit(solution)/shard_map/ppermute | solution.py:22
  42.2 0.0 collective-permute-done
  42.2 2.1 %pad_maximum_fusion.white_ref = bf16[3,2,48,2048]{3,2,1,0:T(8,128)(2,1)} fusion(bf16[1,2,48,2048]{3,2,1,0:T(8,128)(2,1)S(1)} %bitcast.26, bf16[1,2,48,2048]{3,2,1,0:T(8,128)(2,1)S(1)} %bitcast.27, bf16[1,2,48,2048]{3,2,1,0:T(8,128)(2,1)} %bitcast.24), kind=kLoop, calls=%fused_computation.1 | loop fusion | flops 1179648 | bytes 2359296 | tf_op jit(solution)/shard_map/stack | solution.py:148
  44.3 17.6 %shard_map.51 = f32[5,1152,256]{2,1,0:T(8,128)} custom-call(bf16[3,2,48,2048]{3,2,1,0:T(8,128)(2,1)} %pad_maximum_fusion.white_ref, bf16[4096,256]{1,0:T(8,128)(2,1)} %constant.55.clone.table_ref), custom_call_target="tpu_custom_call" | custom-call | tf_op jit(solution)/shard_map/pallas_call | solution.py:137
  61.9 2.4 %slice_bitcast_fusion = f32[1152,256]{1,0:T(8,128)} fusion(f32[5,1152,256]{2,1,0:T(8,128)} %shard_map.51), kind=kLoop, calls=%fused_computation | loop fusion | bytes 2359296 | tf_op jit(solution)/shard_map/squeeze | solution.py:150
  64.3 0.0 reduce-scatter.5.cloned.1.call-update
  64.3 0.0 reduce-scatter.3.cloned.1.call-start
  64.4 4.8 %slice.8 = f32[4,1152,256]{2,1,0:T(8,128)} slice(f32[5,1152,256]{2,1,0:T(8,128)} %shard_map.51), slice={[0:4], [0:1152], [0:256]} | slice | bytes 9437184 | tf_op jit(solution)/shard_map/slice | solution.py:149
  69.2 0.0 copy-start
  69.2 0.0 reduce-scatter.3.cloned.1.call-update
  69.3 0.6 copy-done
  69.9 8.8 %all-gather = s32[8,1,16]{2,1,0:T(1,128)S(1)} all-gather(s32[1,1,16]{2,1,0:T(1,128)S(1)} %bitcast.29), channel_id=1, replica_groups=mesh['hours'=8,'blocks'=4] {'hours'}, dimensions={0}, use_global_device_ids=true | all-gather | bytes 576 | tf_op jit(solution)/shard_map/all_gather | solution.py:155
  78.7 13.4 %all-gather.1 = s32[4,16,8]{1,2,0:T(8,128)S(1)} all-gather(s32[1,16,8]{1,2,0:T(8,128)S(1)} %bitcast.28), channel_id=1, replica_groups=mesh['hours'=8,'blocks'=4] {'blocks'}, dimensions={0}, use_global_device_ids=true | all-gather | bytes 2560 | tf_op jit(solution)/shard_map/all_gather | solution.py:156
  92.0 0.1 reshape.32
  92.1 0.2 fusion.3
  92.4 0.1 fusion.2
  92.5 0.2 broadcast_in_dim.33
  92.6 0.3 stack_reshape_reshape.7
  93.0 0.2 broadcast_in_dim.31
  93.1 0.3 stack_reshape_reshape.6
  93.4 0.1 dynamic_slice.18
  93.5 0.1 broadcast_in_dim.36
  93.6 0.2 reshape_reshape.3
  93.9 0.1 dynamic-slice_maximum_fusion
  93.9 0.1 fusion.1
  94.0 7.6 %reduce-scatter.5.cloned.1.call-done = f32[144,256]{1,0:T(8,128)} async-done(((f32[1152,256]{1,0:T(8,128)}), f32[144,256]{1,0:T(8,128)}) %reduce-scatter.5.cloned.1.call-update) | async-done | bytes 147472 | tf_op jit(solution)/shard_map/reduce_scatter | solution.py:162
  101.6 1.7 divide_bitcast_fusion.1
  103.2 56.1 %reduce-scatter.3.cloned.1.call-done = f32[2,288,256]{2,1,0:T(8,128)} async-done(((f32[2,2304,256]{2,1,0:T(8,128)}), f32[2,288,256]{2,1,0:T(8,128)}) %reduce-scatter.3.cloned.1.call-update) | async-done | bytes 589840 | tf_op jit(solution)/shard_map/reduce_scatter | solution.py:161
  159.3 2.0 %divide_bitcast_fusion = f32[1,2,288,256]{3,2,1,0:T(8,128)} fusion(f32[2,288,256]{2,1,0:T(8,128)} %reduce-scatter.3.cloned.1.call-done, f32[2,288]{1,0:T(2,128)S(1)} %fusion.1), kind=kLoop, calls=%fused_computation.2 | loop fusion | flops 147456 | bytes 1181952 | tf_op jit(solution)/shard_map/broadcast_in_dim | solution.py:192
  (8 shorter events, 0.1 us)
Async XLA Ops:
  7.2 94.4 %reduce-scatter.5.cloned.1.call-start = ((), (), s32[]{:S(2)}) async-start(), calls=%async_computation.3 | async-start | bytes 1327104 | tf_op jit(solution)/shard_map/reduce_scatter | solution.py:162
  12.0 30.2 %collective-permute-start.1 = (bf16[2,48,2048]{2,1,0:T(8,128)(2,1)}, bf16[2,48,2048]{2,1,0:T(8,128)(2,1)S(1)}, u32[]{:S(2)}, u32[]{:S(2)}) collective-permute-start(bf16[2,48,2048]{2,1,0:T(8,128)(2,1)} %shard_map.50), channel_id=1, source_target_pairs={{2,0},{3,1},{0,2},{1,3},{6,4},{7,5},{4,6},{5,7},{10,8},{11,9},{8,1... | collective-permute-start | bytes 1179656 | tf_op jit(solution)/shard_map/ppermute | solution.py:22
  16.0 26.2 %collective-permute-start = (bf16[2,48,2048]{2,1,0:T(8,128)(2,1)}, bf16[2,48,2048]{2,1,0:T(8,128)(2,1)S(1)}, u32[]{:S(2)}, u32[]{:S(2)}) collective-permute-start(bf16[2,48,2048]{2,1,0:T(8,128)(2,1)} %shard_map.50), channel_id=1, source_target_pairs={{3,0},{0,1},{1,2},{2,3},{7,4},{4,5},{5,6},{6,7},{11,8},{8,9},{9,10... | collective-permute-start | bytes 1179656 | tf_op jit(solution)/shard_map/ppermute | solution.py:22
  64.3 95.0 %reduce-scatter.3.cloned.1.call-start = ((), (), s32[]{:S(2)}) async-start(), calls=%async_computation.2 | async-start | bytes 5308416 | tf_op jit(solution)/shard_map/reduce_scatter | solution.py:161
  69.2 0.7 copy-start
Sparse Core Ops, SparseCore 0:
  64.5 37.0 reduce-scatter.4
  105.4 53.8 reduce-scatter.2

commit v2 on v1

--- a/solution.py
+++ b/solution.py
@@ -192,14 +192,327 @@
     return (near_stack[None], far_stack[None])
 
 
+def fused_kernel(
+    sizes, spectra_ref, valid_ref, tile_ref, table_ref, near_ref, far_ref,
+    white, rows, tile0, tile1, acc, masks, all_masks,
+    near_part, far_part, near_sib, far_sib, near_pair, far_pair, near_in, far_in,
+    z_send, z_recv, m_send, m_recv, h_send, h_recv, s_send, s_recv, c_send, c_recv,
+):
+    block_count, hour_devices = sizes
+    chips = hour_devices // 2
+    trace_count = white.shape[2]
+    half = trace_count // 2
+    near_share = near_ref.shape[1]
+    far_share = far_ref.shape[0]
+    me = lax.axis_index("hours")
+    block = lax.axis_index("blocks")
+    core = lax.rem(me, 2)
+    chip = me // 2
+    other = 1 - core
+    is_lower = block < block_count // 2
+    following = lax.rem(block + 1, block_count)
+    partner = lax.rem(block + 2, block_count)
+
+    def remote(src, dst, send, recv, device):
+        return pltpu.make_async_remote_copy(
+            src_ref=src, dst_ref=dst, send_sem=send, recv_sem=recv,
+            device_id=device, device_id_type=pl.DeviceIdType.MESH,
+        )
+
+    barrier = pltpu.get_barrier_semaphore()
+    for step in range(1, hour_devices):
+        pl.semaphore_signal(
+            barrier, inc=1, device_id={"hours": lax.rem(me + step, hour_devices)},
+            device_id_type=pl.DeviceIdType.MESH,
+        )
+    for step in range(1, block_count):
+        pl.semaphore_signal(
+            barrier, inc=1, device_id={"blocks": lax.rem(block + step, block_count)},
+            device_id_type=pl.DeviceIdType.MESH,
+        )
+
+    def store(part, lanes, value):
+        white[0, part, :, lanes] = value
+        rows[part, :trace_count, lanes] = value.astype(jnp.float32)
+
+    whiten_into(spectra_ref, valid_ref, store)
+    masks[0] = tile_ref[...]
+    pl.semaphore_wait(barrier, hour_devices + block_count - 2)
+
+    mask_copies = [
+        remote(masks.at[0], masks.at[i + 1], m_send.at[i], m_recv.at[i], {"blocks": to})
+        for i, to in enumerate((following, partner))
+    ]
+    near_copy = remote(
+        white.at[0], white.at[1], z_send.at[0], z_recv.at[0], {"blocks": following}
+    )
+    full_copy = remote(
+        white.at[0], white.at[2], z_send.at[1], z_recv.at[1], {"blocks": partner}
+    )
+    lead = half // 16 * 16
+    upper_part = pl.ds(lead, trace_count - lead)
+    half_copy = remote(
+        white.at[0, :, upper_part], white.at[2, :, upper_part],
+        z_send.at[1], z_recv.at[1], {"blocks": partner},
+    )
+    for copy in mask_copies:
+        copy.start()
+    near_copy.start()
+
+    @pl.when(is_lower)
+    def _():
+        half_copy.start()
+
+    @pl.when(jnp.logical_not(is_lower))
+    def _():
+        full_copy.start()
+
+    def hour_copy(step):
+        return remote(
+            masks, all_masks.at[me], h_send.at[step - 1], h_recv.at[step - 1],
+            {"hours": lax.rem(me + step, hour_devices)},
+        )
+
+    def sibling_near(unit):
+        at = pl.ds(lax.rem(unit, 2) * (chips // 2), chips // 2)
+        r = unit // 2
+        return remote(
+            near_part.at[r, other, at], near_sib.at[r, at],
+            s_send.at[unit], s_recv.at[unit], {"hours": chip * 2 + other},
+        )
+
+    sibling_far = remote(
+        far_part.at[other], far_sib, s_send.at[4], s_recv.at[4], {"hours": chip * 2 + other}
+    )
+
+    def chip_near(r, target):
+        return remote(
+            near_pair.at[r, target], near_in.at[r, chip],
+            c_send.at[r, target], c_recv.at[r, chip], {"hours": target * 2 + core},
+        )
+
+    def chip_far(target):
+        return remote(
+            far_pair.at[target], far_in.at[chip],
+            c_send.at[2, target], c_recv.at[2, chip], {"hours": target * 2 + core},
+        )
+
+    def reduce_near(unit):
+        sibling_near(unit).wait_recv()
+        r = unit // 2
+        for i in range(chips // 2):
+            target = lax.rem(unit, 2) * (chips // 2) + i
+
+            @pl.when(target != chip)
+            def _():
+                near_pair[r, target] = (
+                    near_part[r, core, target].astype(jnp.float32)
+                    + near_sib[r, target].astype(jnp.float32)
+                ).astype(jnp.bfloat16)
+                chip_near(r, target).start()
+
+    def one_unit(unit, carry):
+        near = unit < 4
+
+        @pl.when(unit == 2)
+        def _():
+            for copy in mask_copies:
+                copy.wait_recv()
+            all_masks[me] = masks[...]
+            for step in range(1, hour_devices):
+                hour_copy(step).start()
+            near_copy.wait_recv()
+
+        @pl.when(jnp.logical_and(unit == 4, is_lower))
+        def _():
+            full_copy.wait_recv()
+            rows[:, trace_count:, :] = rows[:, :half, :]
+
+        @pl.when(jnp.logical_and(unit == 4, jnp.logical_not(is_lower)))
+        def _():
+            half_copy.wait_recv()
+            for part in range(2):
+                value = white[2, part, lead:, :].astype(jnp.float32)
+                rows[part, trace_count:, :] = value[half - lead :]
+
+        row_start = jnp.where(near, lax.rem(unit, 2) * half, trace_count)
+        panel = jnp.where(near, unit // 2, jnp.where(is_lower, 2, 0))
+        correlate_unit(rows, row_start, half, white, panel, table_ref, acc, (tile0, tile1))
+
+        @pl.when(near)
+        def _():
+            for i in range(hour_devices // 2):
+                target = lax.rem(unit, 2) * (chips // 2) + i // 2
+                near_part[unit // 2, i % 2, target] = acc[
+                    i * near_share : (i + 1) * near_share, :
+                ].astype(jnp.bfloat16)
+            sibling_near(unit).start()
+
+        @pl.when(jnp.logical_not(near))
+        def _():
+            for i in range(hour_devices):
+                far_part[i % 2, i // 2] = acc[
+                    i * far_share : (i + 1) * far_share, :
+                ].astype(jnp.bfloat16)
+            sibling_far.start()
+
+        @pl.when(unit >= 1)
+        def _():
+            reduce_near(unit - 1)
+
+        return carry
+
+    lax.fori_loop(0, 5, one_unit, 0)
+
+    sibling_far.wait_recv()
+    for step in range(1, chips):
+        target = lax.rem(chip + step, chips)
+        far_pair[target] = (
+            far_part[core, target].astype(jnp.float32) + far_sib[target].astype(jnp.float32)
+        ).astype(jnp.bfloat16)
+        chip_far(target).start()
+
+    for step in range(1, hour_devices):
+        hour_copy(step).wait()
+
+    def counts(row_mask, row_start, row_count, col_mask):
+        shape = (row_count, trace_count, 128)
+        lane = lax.broadcasted_iota(jnp.int32, shape, 2)
+        row = lax.broadcasted_iota(jnp.int32, shape, 0) + row_start
+        col = lax.broadcasted_iota(jnp.int32, shape, 1)
+        flat = (row_count * trace_count, 128)
+
+        def picked(index, mask):
+            chosen = jnp.where(lane == index, 1.0, 0.0).reshape(flat)
+            return lax.dot_general(
+                chosen, mask, (((1,), (1,)), ((), ())), preferred_element_type=jnp.float32
+            )
+
+        both = picked(row, row_mask) * picked(col, col_mask)
+        return jnp.maximum(jnp.sum(both, axis=1, keepdims=True), 1.0)
+
+    row_share = near_share // trace_count
+    own_mask = all_masks[:, 0, 0, :]
+    near_counts = [
+        counts(own_mask, me * row_share, row_share, all_masks[:, r, 0, :]) for r in range(2)
+    ]
+    far_mask = all_masks[:, 2, 0, :]
+    far_count = counts(
+        jnp.where(is_lower, own_mask, far_mask),
+        me * (row_share // 2) + jnp.where(is_lower, 0, half),
+        row_share // 2,
+        jnp.where(is_lower, far_mask, own_mask),
+    )
+
+    def chip_near_arrival(r, source):
+        return remote(
+            near_pair.at[r, source], near_in.at[r, source],
+            c_send.at[r, source], c_recv.at[r, source], {"hours": source * 2 + core},
+        )
+
+    def chip_far_arrival(source):
+        return remote(
+            far_pair.at[source], far_in.at[source],
+            c_send.at[2, source], c_recv.at[2, source], {"hours": source * 2 + core},
+        )
+
+    for r in range(2):
+        total = near_part[r, core, chip].astype(jnp.float32) + near_sib[r, chip].astype(
+            jnp.float32
+        )
+        for step in range(1, chips):
+            source = lax.rem(chip + step, chips)
+            chip_near_arrival(r, source).wait()
+            total = total + near_in[r, source].astype(jnp.float32)
+        near_ref[r] = total / near_counts[r]
+    total = far_part[core, chip].astype(jnp.float32) + far_sib[chip].astype(jnp.float32)
+    for step in range(1, chips):
+        source = lax.rem(chip + step, chips)
+        chip_far_arrival(source).wait()
+        total = total + far_in[source].astype(jnp.float32)
+    far_ref[...] = total / far_count
+
+    for copy in mask_copies:
+        copy.wait_send()
+    near_copy.wait_send()
+
+    @pl.when(is_lower)
+    def _():
+        half_copy.wait_send()
+
+    @pl.when(jnp.logical_not(is_lower))
+    def _():
+        full_copy.wait_send()
+
+    for unit in range(4):
+        sibling_near(unit).wait_send()
+    sibling_far.wait_send()
+
+
+def on_device_fused(table, spectra, validity):
+    hour_count, station_count, comp_count, part_count, freq_count = spectra.shape
+    trace_count = station_count * comp_count
+    half = trace_count // 2
+    block_count = lax.axis_size("blocks")
+    hour_devices = lax.axis_size("hours")
+    chips = hour_devices // 2
+    pair_rows = half * trace_count
+    near_share = 2 * pair_rows // hour_devices
+    far_share = pair_rows // hour_devices
+    valid_f = jnp.repeat(validity.reshape(-1).astype(jnp.float32), comp_count)
+    tile = jnp.broadcast_to(jnp.pad(valid_f, (0, 128 - trace_count))[None, :], (8, 128))
+    near, far = pl.pallas_call(
+        functools.partial(fused_kernel, (block_count, hour_devices)),
+        out_shape=(
+            jax.ShapeDtypeStruct((2, near_share, LAGS), jnp.float32),
+            jax.ShapeDtypeStruct((far_share, LAGS), jnp.float32),
+        ),
+        in_specs=[pl.BlockSpec(memory_space=pltpu.VMEM)] * 4,
+        out_specs=[pl.BlockSpec(memory_space=pltpu.VMEM)] * 2,
+        scratch_shapes=[
+            pltpu.VMEM((3, part_count, trace_count, freq_count), jnp.bfloat16),
+            pltpu.VMEM((part_count, trace_count + half, freq_count), jnp.float32),
+            pltpu.VMEM((pair_rows, 2 * CHUNK), jnp.bfloat16),
+            pltpu.VMEM((pair_rows, 2 * CHUNK), jnp.bfloat16),
+            pltpu.VMEM((pair_rows, LAGS), jnp.float32),
+            pltpu.VMEM((3, 8, 128), jnp.float32),
+            pltpu.VMEM((hour_devices, 3, 8, 128), jnp.float32),
+            pltpu.VMEM((2, 2, chips, near_share, LAGS), jnp.bfloat16),
+            pltpu.VMEM((2, chips, far_share, LAGS), jnp.bfloat16),
+            pltpu.VMEM((2, chips, near_share, LAGS), jnp.bfloat16),
+            pltpu.VMEM((chips, far_share, LAGS), jnp.bfloat16),
+            pltpu.VMEM((2, chips, near_share, LAGS), jnp.bfloat16),
+            pltpu.VMEM((chips, far_share, LAGS), jnp.bfloat16),
+            pltpu.VMEM((2, chips, near_share, LAGS), jnp.bfloat16),
+            pltpu.VMEM((chips, far_share, LAGS), jnp.bfloat16),
+            pltpu.SemaphoreType.DMA((2,)),
+            pltpu.SemaphoreType.DMA((2,)),
+            pltpu.SemaphoreType.DMA((2,)),
+            pltpu.SemaphoreType.DMA((2,)),
+            pltpu.SemaphoreType.DMA((hour_devices - 1,)),
+            pltpu.SemaphoreType.DMA((hour_devices - 1,)),
+            pltpu.SemaphoreType.DMA((5,)),
+            pltpu.SemaphoreType.DMA((5,)),
+            pltpu.SemaphoreType.DMA((3, chips)),
+            pltpu.SemaphoreType.DMA((3, chips)),
+        ],
+        compiler_params=pltpu.CompilerParams(
+            vmem_limit_bytes=48 * 1024 * 1024, collective_id=0, has_side_effects=True
+        ),
+    )(spectra.reshape(trace_count, part_count, freq_count), valid_f[:, None], tile, table)
+    return near[None], far[None]
+
+
 def solution(mesh):
     in_specs = (P("hours", "blocks", None, None, None), P("hours", "blocks"))
     out_specs = (P("blocks", None, "hours", None), P("blocks", "hours", None))
 
     def run(spectra, validity):
         table = chunked_table(spectra.shape[-1], LAGS)
+        fits = mesh.shape["hours"] == 8 and mesh.shape["blocks"] == 4
+        device_part = on_device_fused if fits else on_device
         return jax.shard_map(
-            lambda *args: on_device(jnp.asarray(table), *args),
+            lambda *args: device_part(jnp.asarray(table), *args),
             mesh=mesh, in_specs=in_specs, out_specs=out_specs, check_vma=False,
         )(spectra, validity)
 

time: 169 us -> 51.7 us (0.31)
  waiting for transfers between devices: 88.3 us -> 0 us
  Pallas kernels: 21 us -> 45.8 us
  blocking collectives: 22.1 us -> 0 us
  between operations: 14.2 us -> 0.66 us
  other arithmetic: 6.66 us -> 0.66 us
  starting transfers between devices: 5.69 us -> 0 us
  local copies, waits for them, and re-layouts: 10.1 us -> 4.44 us
    reduce_scatter x2 -> x0, waiting for transfers between devices: 63.6 us -> none  [the longest x1 56.1 us: on_device(): lax.psum_scatter(near_terms, 'hours', scatter_dimension=1, tiled=True)]
    pallas_call x2 -> x1, Pallas kernels: 21 us -> 45.8 us  [on_device_fused(): pl.pallas_call(functools.partial(fused_kernel, (block_count, hour_devices...]
    ppermute x2 -> x0, waiting for transfers between devices: 24.6 us -> none  [passed_along(): return lax.ppermute(block, axis, route)]
    all_gather x2 -> x0, blocking collectives: 22.1 us -> none  [the longest x1 13.4 us: on_device(): lax.all_gather(hour_masks, 'blocks', axis=1, tiled=True).astype(jnp.float32)]
    ppermute x2 -> x0, starting transfers between devices: 5.61 us -> none  [passed_along(): return lax.ppermute(block, axis, route)]
    slice x1 -> x0, local copies, waits for them, and re-layouts: 4.82 us -> none  [on_device(): near_terms = sums[:4].reshape(near_rounds, 2 * pair_rows, LAGS)]
    broadcast_in_dim x2 -> x0, other arithmetic: 3.69 us -> none  [on_device(): return (near_stack[None], far_stack[None])]
    unnamed x2 -> x6, local copies, waits for them, and re-layouts: 0.57 us -> 4.2 us
  transfers between devices with their start and end apart: 4 -> 0, of which waited for: 3 -> 0; matrix products, arithmetic and copies ran while one was open for 5% -> 0% of each run, Pallas kernels for 0% -> 0%
where the time goes in v2:
time: 51.7 us; the launch traced here: 51.5 us
  Pallas kernels  45.8 us (89%)
  local copies, waits for them, and re-layouts  4.44 us (9%)
  other arithmetic  0.66 us (1%)
  between operations  0.66 us (1%)
    pallas_call x1, Pallas kernels, on_device_fused(): pl.pallas_call(functools.partial(fused_kernel, (block_count, hour_devices...  45.8 us
    unnamed x6, local copies, waits for them, and re-layouts  4.2 us

profile of v2, /device:TPU:0, one launch (start us, length us, event | category | flops | bytes accessed | tf_op | source)
XLA Modules:
  0.0 51.5 jit_solution(7623809192680955992)
XLA Ops:
  0.6 0.7 %convert_bitcast_fusion = f32[16]{0:T(128)S(1)} fusion(s32[1,16]{1,0:T(1,128)} %param.4), kind=kLoop, calls=%fused_computation | loop fusion | flops 16 | bytes 128 | tf_op jit(solution)/shard_map/convert_element_type | solution.py:462
  1.3 0.1 broadcast_in_dim.15
  1.4 0.1 reshape.14
  1.5 0.1 broadcast_in_dim_reshape.4.valid_ref
  1.5 0.0 copy-start
  1.5 1.6 %copy-done = bf16[4096,256]{1,0:T(8,128)(2,1)S(1)} copy-done((bf16[4096,256]{1,0:T(8,128)(2,1)S(1)}, bf16[4096,256]{1,0:T(8,128)(2,1)}, u32[]{:S(2)}) %copy-start) | copy-done | bytes 2097176
  3.1 0.0 copy-start.1
  3.1 1.1 %copy-done.1 = f32[1,16,3,2,2048]{4,3,2,1,0:T(2,128)S(1)} copy-done((f32[1,16,3,2,2048]{4,3,2,1,0:T(2,128)S(1)}, f32[1,16,3,2,2048]{4,3,2,1,0:T(2,128)}, u32[]{:S(2)}) %copy-start.1) | copy-done | bytes 786456
  4.3 45.8 %shard_map.50 = (f32[2,288,256]{2,1,0:T(8,128)S(1)}, f32[144,256]{1,0:T(8,128)S(1)}) custom-call(f32[48,2,2048]{2,1,0:T(2,128)S(1)} %bitcast.5, f32[48,1]{1,0:T(8,128)S(1)} %broadcast_in_dim_reshape.4.valid_ref, f32[8,128]{1,0:T(8,128)S(1)} %broadcast_in_dim.16.tile_ref, bf16[4096,256]{1,0:T(8,128)(2,1)S(1)} %copy-done), custom_call_target="tpu_custom_call" | custom-call | tf_op jit(solution)/shard_map/pallas_call | solution.py:464
  50.1 0.8 %copy.9 = f32[1,2,288,256]{3,2,1,0:T(8,128)} copy(f32[1,2,288,256]{3,2,1,0:T(8,128)S(1)} %bitcast.6) | data formatting | bytes 1179648
  50.9 0.7 %copy.10 = f32[1,144,256]{2,1,0:T(8,128)} copy(f32[1,144,256]{2,1,0:T(8,128)S(1)} %bitcast.7) | data formatting | bytes 294912
  (2 shorter events, 0.0 us)
Async XLA Ops:
  1.5 1.6 %copy-start = (bf16[4096,256]{1,0:T(8,128)(2,1)S(1)}, bf16[4096,256]{1,0:T(8,128)(2,1)}, u32[]{:S(2)}) copy-start(bf16[4096,256]{1,0:T(8,128)(2,1)} %constant.5.clone.table_ref) | copy-start | bytes 6291460
  3.1 1.1 %copy-start.1 = (f32[1,16,3,2,2048]{4,3,2,1,0:T(2,128)S(1)}, f32[1,16,3,2,2048]{4,3,2,1,0:T(2,128)}, u32[]{:S(2)}) copy-start(f32[1,16,3,2,2048]{4,3,2,1,0:T(2,128)} %param.3) | copy-start | bytes 2359300

commit v3 on v2

--- a/solution.py
+++ b/solution.py
@@ -193,10 +193,11 @@
 
 
 def fused_kernel(
-    sizes, spectra_ref, valid_ref, tile_ref, table_ref, near_ref, far_ref,
-    white, rows, tile0, tile1, acc, masks, all_masks,
+    sizes, spectra_ref, valid_ref, tile_ref, table_hbm, near_ref, far_ref,
+    table_ref, white, rows, tile0, tile1, acc, masks, all_masks,
     near_part, far_part, near_sib, far_sib, near_pair, far_pair, near_in, far_in,
-    z_send, z_recv, m_send, m_recv, h_send, h_recv, s_send, s_recv, c_send, c_recv,
+    z_send, z_recv, f_send, t_sem, m_send, m_recv, h_send, h_recv, s_send, s_recv,
+    c_send, c_recv,
 ):
     block_count, hour_devices = sizes
     chips = hour_devices // 2
@@ -219,6 +220,8 @@
             device_id=device, device_id_type=pl.DeviceIdType.MESH,
         )
 
+    table_copy = pltpu.make_async_copy(table_hbm, table_ref, t_sem)
+    table_copy.start()
     barrier = pltpu.get_barrier_semaphore()
     for step in range(1, hour_devices):
         pl.semaphore_signal(
@@ -243,29 +246,58 @@
         remote(masks.at[0], masks.at[i + 1], m_send.at[i], m_recv.at[i], {"blocks": to})
         for i, to in enumerate((following, partner))
     ]
-    near_copy = remote(
-        white.at[0], white.at[1], z_send.at[0], z_recv.at[0], {"blocks": following}
-    )
-    full_copy = remote(
-        white.at[0], white.at[2], z_send.at[1], z_recv.at[1], {"blocks": partner}
-    )
     lead = half // 16 * 16
     upper_part = pl.ds(lead, trace_count - lead)
-    half_copy = remote(
-        white.at[0, :, upper_part], white.at[2, :, upper_part],
-        z_send.at[1], z_recv.at[1], {"blocks": partner},
-    )
+    parts = range(2)
+    near_copies = [
+        remote(
+            white.at[0, p], white.at[1, p], z_send.at[p], z_recv.at[p], {"blocks": following}
+        )
+        for p in parts
+    ]
+    full_copies = [
+        remote(
+            white.at[0, p], white.at[2, p], z_send.at[2 + p], z_recv.at[2 + p],
+            {"blocks": partner},
+        )
+        for p in parts
+    ]
+    half_copies = [
+        remote(
+            white.at[0, p, upper_part], white.at[2, p, upper_part],
+            z_send.at[2 + p], z_recv.at[2 + p], {"blocks": partner},
+        )
+        for p in parts
+    ]
+    last = block == block_count - 1
+    relay = block == 1
+    relay_copies = [
+        remote(
+            white.at[2, p], white.at[1, p], f_send.at[p], z_recv.at[p],
+            {"blocks": lax.rem(block + block_count - 1, block_count)},
+        )
+        for p in parts
+    ]
     for copy in mask_copies:
         copy.start()
-    near_copy.start()
-
-    @pl.when(is_lower)
+
+    @pl.when(last)
     def _():
-        half_copy.start()
-
-    @pl.when(jnp.logical_not(is_lower))
+        for copy in full_copies:
+            copy.start()
+
+    @pl.when(jnp.logical_not(last))
     def _():
-        full_copy.start()
+        for copy in near_copies:
+            copy.start()
+
+    def relay_part(p):
+        @pl.when(relay)
+        def _():
+            full_copies[p].wait_recv()
+            relay_copies[p].start()
+
+    table_copy.wait()
 
     def hour_copy(step):
         return remote(
@@ -274,7 +306,7 @@
         )
 
     def sibling_near(unit):
-        at = pl.ds(lax.rem(unit, 2) * (chips // 2), chips // 2)
+        at = pl.ds((unit % 2) * (chips // 2), chips // 2)
         r = unit // 2
         return remote(
             near_part.at[r, other, at], near_sib.at[r, at],
@@ -301,7 +333,7 @@
         sibling_near(unit).wait_recv()
         r = unit // 2
         for i in range(chips // 2):
-            target = lax.rem(unit, 2) * (chips // 2) + i
+            target = (unit % 2) * (chips // 2) + i
 
             @pl.when(target != chip)
             def _():
@@ -314,26 +346,52 @@
     def one_unit(unit, carry):
         near = unit < 4
 
+        @pl.when(unit == 1)
+        def _():
+            relay_part(0)
+
         @pl.when(unit == 2)
         def _():
+            relay_part(1)
+
+            @pl.when(is_lower)
+            def _():
+                for copy in half_copies:
+                    copy.start()
+
+            @pl.when(jnp.logical_not(jnp.logical_or(is_lower, last)))
+            def _():
+                for copy in full_copies:
+                    copy.start()
+
             for copy in mask_copies:
                 copy.wait_recv()
             all_masks[me] = masks[...]
             for step in range(1, hour_devices):
                 hour_copy(step).start()
-            near_copy.wait_recv()
-
-        @pl.when(jnp.logical_and(unit == 4, is_lower))
-        def _():
-            full_copy.wait_recv()
-            rows[:, trace_count:, :] = rows[:, :half, :]
-
-        @pl.when(jnp.logical_and(unit == 4, jnp.logical_not(is_lower)))
-        def _():
-            half_copy.wait_recv()
-            for part in range(2):
-                value = white[2, part, lead:, :].astype(jnp.float32)
-                rows[part, trace_count:, :] = value[half - lead :]
+            reduce_near(1)
+            for copy in near_copies:
+                copy.wait_recv()
+
+        @pl.when(unit == 4)
+        def _():
+            reduce_near(3)
+
+            @pl.when(block == 0)
+            def _():
+                for copy in full_copies:
+                    copy.wait_recv()
+
+            @pl.when(is_lower)
+            def _():
+                rows[:, trace_count:, :] = rows[:, :half, :]
+
+            @pl.when(jnp.logical_not(is_lower))
+            def _():
+                for p in parts:
+                    half_copies[p].wait_recv()
+                    value = white[2, p, lead:, :].astype(jnp.float32)
+                    rows[p, trace_count:, :] = value[half - lead :]
 
         row_start = jnp.where(near, lax.rem(unit, 2) * half, trace_count)
         panel = jnp.where(near, unit // 2, jnp.where(is_lower, 2, 0))
@@ -356,7 +414,7 @@
                 ].astype(jnp.bfloat16)
             sibling_far.start()
 
-        @pl.when(unit >= 1)
+        @pl.when(jnp.logical_or(unit == 1, unit == 3))
         def _():
             reduce_near(unit - 1)
 
@@ -434,15 +492,26 @@
 
     for copy in mask_copies:
         copy.wait_send()
-    near_copy.wait_send()
+
+    @pl.when(jnp.logical_not(last))
+    def _():
+        for copy in near_copies:
+            copy.wait_send()
+
+    @pl.when(relay)
+    def _():
+        for copy in relay_copies:
+            copy.wait_send()
 
     @pl.when(is_lower)
     def _():
-        half_copy.wait_send()
+        for copy in half_copies:
+            copy.wait_send()
 
     @pl.when(jnp.logical_not(is_lower))
     def _():
-        full_copy.wait_send()
+        for copy in full_copies:
+            copy.wait_send()
 
     for unit in range(4):
         sibling_near(unit).wait_send()
@@ -467,9 +536,11 @@
             jax.ShapeDtypeStruct((2, near_share, LAGS), jnp.float32),
             jax.ShapeDtypeStruct((far_share, LAGS), jnp.float32),
         ),
-        in_specs=[pl.BlockSpec(memory_space=pltpu.VMEM)] * 4,
+        in_specs=[pl.BlockSpec(memory_space=pltpu.VMEM)] * 3
+        + [pl.BlockSpec(memory_space=pl.ANY)],
         out_specs=[pl.BlockSpec(memory_space=pltpu.VMEM)] * 2,
         scratch_shapes=[
+            pltpu.VMEM(table.shape, jnp.bfloat16),
             pltpu.VMEM((3, part_count, trace_count, freq_count), jnp.bfloat16),
             pltpu.VMEM((part_count, trace_count + half, freq_count), jnp.float32),
             pltpu.VMEM((pair_rows, 2 * CHUNK), jnp.bfloat16),
@@ -485,8 +556,10 @@
             pltpu.VMEM((chips, far_share, LAGS), jnp.bfloat16),
             pltpu.VMEM((2, chips, near_share, LAGS), jnp.bfloat16),
             pltpu.VMEM((chips, far_share, LAGS), jnp.bfloat16),
+            pltpu.SemaphoreType.DMA((4,)),
+            pltpu.SemaphoreType.DMA((4,)),
             pltpu.SemaphoreType.DMA((2,)),
-            pltpu.SemaphoreType.DMA((2,)),
+            pltpu.SemaphoreType.DMA,
             pltpu.SemaphoreType.DMA((2,)),
             pltpu.SemaphoreType.DMA((2,)),
             pltpu.SemaphoreType.DMA((hour_devices - 1,)),

time: 51.7 us -> 53.5 us (1.035)
  Pallas kernels: 45.8 us -> 47.4 us
    pallas_call x1, Pallas kernels: 45.8 us -> 47.4 us  [on_device_fused(): pl.pallas_call(functools.partial(fused_kernel, (block_count, hour_devices...]
where the time goes in v3:
time: 53.5 us; the launch traced here: 53.2 us
  Pallas kernels  47.4 us (89%)
  local copies, waits for them, and re-layouts  4.44 us (8%)
  other arithmetic  0.66 us (1%)
  between operations  0.66 us (1%)
    pallas_call x1, Pallas kernels, on_device_fused(): pl.pallas_call(functools.partial(fused_kernel, (block_count, hour_devices...  47.4 us
    unnamed x6, local copies, waits for them, and re-layouts  4.2 us

profile of v3, /device:TPU:0, one launch (start us, length us, event | category | flops | bytes accessed | tf_op | source)
XLA Modules:
  0.0 53.2 jit_solution(11277581300960022037)
XLA Ops:
  0.6 0.7 %convert_bitcast_fusion = f32[16]{0:T(128)S(1)} fusion(s32[1,16]{1,0:T(1,128)} %param.4), kind=kLoop, calls=%fused_computation | loop fusion | flops 16 | bytes 128 | tf_op jit(solution)/shard_map/convert_element_type | solution.py:531
  1.3 0.1 broadcast_in_dim.15
  1.4 0.1 reshape.14
  1.5 0.1 broadcast_in_dim_reshape.4.valid_ref
  1.5 0.0 copy-start
  1.5 1.6 %copy-done = bf16[4096,256]{1,0:T(8,128)(2,1)S(1)} copy-done((bf16[4096,256]{1,0:T(8,128)(2,1)S(1)}, bf16[4096,256]{1,0:T(8,128)(2,1)}, u32[]{:S(2)}) %copy-start) | copy-done | bytes 2097176
  3.1 0.0 copy-start.1
  3.1 1.1 %copy-done.1 = f32[1,16,3,2,2048]{4,3,2,1,0:T(2,128)S(1)} copy-done((f32[1,16,3,2,2048]{4,3,2,1,0:T(2,128)S(1)}, f32[1,16,3,2,2048]{4,3,2,1,0:T(2,128)}, u32[]{:S(2)}) %copy-start.1) | copy-done | bytes 786456
  4.3 47.4 %shard_map.50 = (f32[2,288,256]{2,1,0:T(8,128)S(1)}, f32[144,256]{1,0:T(8,128)S(1)}) custom-call(f32[48,2,2048]{2,1,0:T(2,128)S(1)} %bitcast.5, f32[48,1]{1,0:T(8,128)S(1)} %broadcast_in_dim_reshape.4.valid_ref, f32[8,128]{1,0:T(8,128)S(1)} %broadcast_in_dim.16.tile_ref, bf16[4096,256]{1,0:T(8,128)(2,1)S(1)} %copy-done), custom_call_target="tpu_custom_call" | custom-call | tf_op jit(solution)/shard_map/pallas_call | solution.py:533
  51.7 0.8 %copy.9 = f32[1,2,288,256]{3,2,1,0:T(8,128)} copy(f32[1,2,288,256]{3,2,1,0:T(8,128)S(1)} %bitcast.6) | data formatting | bytes 1179648
  52.5 0.7 %copy.10 = f32[1,144,256]{2,1,0:T(8,128)} copy(f32[1,144,256]{2,1,0:T(8,128)S(1)} %bitcast.7) | data formatting | bytes 294912
  (2 shorter events, 0.0 us)
Async XLA Ops:
  1.5 1.6 %copy-start = (bf16[4096,256]{1,0:T(8,128)(2,1)S(1)}, bf16[4096,256]{1,0:T(8,128)(2,1)}, u32[]{:S(2)}) copy-start(bf16[4096,256]{1,0:T(8,128)(2,1)} %constant.5.clone.table_hbm) | copy-start | bytes 6291460
  3.1 1.1 %copy-start.1 = (f32[1,16,3,2,2048]{4,3,2,1,0:T(2,128)S(1)}, f32[1,16,3,2,2048]{4,3,2,1,0:T(2,128)}, u32[]{:S(2)}) copy-start(f32[1,16,3,2,2048]{4,3,2,1,0:T(2,128)} %param.3) | copy-start | bytes 2359300

commit v4 on v3

--- a/solution.py
+++ b/solution.py
@@ -270,31 +270,24 @@
         for p in parts
     ]
     last = block == block_count - 1
-    relay = block == 1
+    relay = block == 0
     relay_copies = [
         remote(
-            white.at[2, p], white.at[1, p], f_send.at[p], z_recv.at[p],
-            {"blocks": lax.rem(block + block_count - 1, block_count)},
+            white.at[1, p], white.at[2, p], f_send.at[p], z_recv.at[2 + p],
+            {"blocks": following},
         )
         for p in parts
     ]
     for copy in mask_copies:
         copy.start()
 
-    @pl.when(last)
-    def _():
-        for copy in full_copies:
-            copy.start()
-
-    @pl.when(jnp.logical_not(last))
-    def _():
-        for copy in near_copies:
-            copy.start()
+    for copy in near_copies:
+        copy.start()
 
     def relay_part(p):
         @pl.when(relay)
         def _():
-            full_copies[p].wait_recv()
+            near_copies[p].wait_recv()
             relay_copies[p].start()
 
     table_copy.wait()
@@ -370,20 +363,20 @@
             for step in range(1, hour_devices):
                 hour_copy(step).start()
             reduce_near(1)
-            for copy in near_copies:
-                copy.wait_recv()
+
+            @pl.when(jnp.logical_not(relay))
+            def _():
+                for copy in near_copies:
+                    copy.wait_recv()
 
         @pl.when(unit == 4)
         def _():
             reduce_near(3)
 
-            @pl.when(block == 0)
+            @pl.when(is_lower)
             def _():
                 for copy in full_copies:
                     copy.wait_recv()
-
-            @pl.when(is_lower)
-            def _():
                 rows[:, trace_count:, :] = rows[:, :half, :]
 
             @pl.when(jnp.logical_not(is_lower))
@@ -493,10 +486,8 @@
     for copy in mask_copies:
         copy.wait_send()
 
-    @pl.when(jnp.logical_not(last))
-    def _():
-        for copy in near_copies:
-            copy.wait_send()
+    for copy in near_copies:
+        copy.wait_send()
 
     @pl.when(relay)
     def _():
@@ -508,7 +499,7 @@
         for copy in half_copies:
             copy.wait_send()
 
-    @pl.when(jnp.logical_not(is_lower))
+    @pl.when(jnp.logical_not(jnp.logical_or(is_lower, last)))
     def _():
         for copy in full_copies:
             copy.wait_send()

time: 53.5 us -> 42.8 us (0.80)
  the two profiles are of different devices: /device:TPU:0 before, /device:TPU:17 now
where the time goes in v4:
time: 42.8 us; the launch traced here: 42.6 us
  Pallas kernels  36.9 us (86%)
  local copies, waits for them, and re-layouts  4.44 us (10%)
  other arithmetic  0.66 us (2%)
  between operations  0.66 us (2%)
    pallas_call x1, Pallas kernels, on_device_fused(): pl.pallas_call(functools.partial(fused_kernel, (block_count, hour_devices...  36.9 us
    unnamed x6, local copies, waits for them, and re-layouts  4.2 us

profile of v4, /device:TPU:17, one launch (start us, length us, event | category | flops | bytes accessed | tf_op | source)
XLA Modules:
  0.0 42.6 jit_solution(430360890429019102)
XLA Ops:
  0.6 0.7 %convert_bitcast_fusion = f32[16]{0:T(128)S(1)} fusion(s32[1,16]{1,0:T(1,128)} %param.4), kind=kLoop, calls=%fused_computation | loop fusion | flops 16 | bytes 128 | tf_op jit(solution)/shard_map/convert_element_type | solution.py:522
  1.3 0.1 broadcast_in_dim.15
  1.4 0.1 reshape.14
  1.5 0.1 broadcast_in_dim_reshape.4.valid_ref
  1.5 0.0 copy-start
  1.5 1.6 %copy-done = bf16[4096,256]{1,0:T(8,128)(2,1)S(1)} copy-done((bf16[4096,256]{1,0:T(8,128)(2,1)S(1)}, bf16[4096,256]{1,0:T(8,128)(2,1)}, u32[]{:S(2)}) %copy-start) | copy-done | bytes 2097176
  3.1 0.0 copy-start.1
  3.1 1.1 %copy-done.1 = f32[1,16,3,2,2048]{4,3,2,1,0:T(2,128)S(1)} copy-done((f32[1,16,3,2,2048]{4,3,2,1,0:T(2,128)S(1)}, f32[1,16,3,2,2048]{4,3,2,1,0:T(2,128)}, u32[]{:S(2)}) %copy-start.1) | copy-done | bytes 786456
  4.3 36.9 %shard_map.50 = (f32[2,288,256]{2,1,0:T(8,128)S(1)}, f32[144,256]{1,0:T(8,128)S(1)}) custom-call(f32[48,2,2048]{2,1,0:T(2,128)S(1)} %bitcast.5, f32[48,1]{1,0:T(8,128)S(1)} %broadcast_in_dim_reshape.4.valid_ref, f32[8,128]{1,0:T(8,128)S(1)} %broadcast_in_dim.16.tile_ref, bf16[4096,256]{1,0:T(8,128)(2,1)S(1)} %copy-done), custom_call_target="tpu_custom_call" | custom-call | tf_op jit(solution)/shard_map/pallas_call | solution.py:524
  41.2 0.8 %copy.9 = f32[1,2,288,256]{3,2,1,0:T(8,128)} copy(f32[1,2,288,256]{3,2,1,0:T(8,128)S(1)} %bitcast.6) | data formatting | bytes 1179648
  42.0 0.7 %copy.10 = f32[1,144,256]{2,1,0:T(8,128)} copy(f32[1,144,256]{2,1,0:T(8,128)S(1)} %bitcast.7) | data formatting | bytes 294912
  (2 shorter events, 0.0 us)
Async XLA Ops:
  1.5 1.6 %copy-start = (bf16[4096,256]{1,0:T(8,128)(2,1)S(1)}, bf16[4096,256]{1,0:T(8,128)(2,1)}, u32[]{:S(2)}) copy-start(bf16[4096,256]{1,0:T(8,128)(2,1)} %constant.5.clone.table_hbm) | copy-start | bytes 6291460
  3.1 1.1 %copy-start.1 = (f32[1,16,3,2,2048]{4,3,2,1,0:T(2,128)S(1)}, f32[1,16,3,2,2048]{4,3,2,1,0:T(2,128)}, u32[]{:S(2)}) copy-start(f32[1,16,3,2,2048]{4,3,2,1,0:T(2,128)} %param.3) | copy-start | bytes 2359300
